TPU v7x, 32 devices: a whole 2x2x4 slice. The times are simulated.
32 devices in a mesh: sx: 8 (over z, core), sy: 4 (over y, x).
Axes of the slice: x: 2, y: 2, z: 4, core: 2. Of those that a mesh axis runs over, the one named last changes fastest.
Arguments:
- features: bfloat16 [64, 128, 512], P(None, 'sx', 'sy'), may hold values from -6 to 6
- enc_weight: bfloat16 [3, 3, 3, 64, 64], replicated, may hold values from -0.15625 to 0.15625
- enc_bias: float32 [64], replicated, may hold values from -3 to 3
- proj_weight: bfloat16 [64, 512], replicated, may hold values from -0.25 to 0.25
- bottle_weight: bfloat16 [3, 3, 3, 512, 512], P(None, None, None, 'sy'), may hold values from -0.0546875 to 0.0546875
- bottle_bias: float32 [512], P('sy'), may hold values from -3 to 3
- out_weight: bfloat16 [512, 64], P('sy'), may hold values from -0.25 to 0.25
- dec_weight: bfloat16 [3, 3, 3, 64, 64], replicated, may hold values from -0.15625 to 0.15625
- dec_bias: float32 [64], replicated, may hold values from -3 to 3
Outputs:
- decoded: bfloat16 [64, 128, 512], P(None, 'sx', 'sy')
All inputs are finite; a program needn't handle non-finite values.
Results may differ from a plain program's by a relative error of at most 0.009.
Values may be sent and summed in bfloat16 or wider, within the bound.
A program may use at most 64 MiB of HBM per device.

v0:
```python
import jax
import jax.numpy as jnp
from jax import lax
from jax.sharding import PartitionSpec as P

POOL = 8
FZ = 16


layout = ("NCDHW", "DHWOI", "NCDHW")


def padded_2(shard, sides, width):
    for axis, dim in sides:
        size, length = (lax.axis_size(axis), shard.shape[dim])
        up = [(i, (i + 1) % size) for i in range(size - 1)]
        down = [(j, i) for i, j in up]
        last = lax.slice_in_dim(shard, length - width, length, axis=dim)
        first = lax.slice_in_dim(shard, 0, width, axis=dim)
        before = lax.ppermute(last, axis, up)
        after = lax.ppermute(first, axis, down)
        shard = jnp.concatenate([before, shard, after], axis=dim)
    return shard


def convolve(padded, kernel, pad_x, pad_y):
    result = lax.conv_general_dilated(
        padded[None],
        kernel,
        (1, 1, 1),
        ((pad_x, pad_x), (pad_y, pad_y), (1, 1)),
        dimension_numbers=layout,
        preferred_element_type=jnp.float32,
    )
    return result[0]


def interpolate(fine_count, fine_first, coarse_count, coarse_first, coarse_total):
    fine_index = fine_first + jnp.arange(fine_count, dtype=jnp.int32)
    coarse_index = coarse_first + jnp.arange(coarse_count, dtype=jnp.int32)
    numerator = 2 * fine_index + 1 - POOL
    low_cell = jnp.floor_divide(numerator, 2 * POOL)
    weight_high = (numerator - 2 * POOL * low_cell).astype(jnp.float32) / jnp.float32(2 * POOL)
    weight_high = jnp.where(low_cell < 0, jnp.float32(0.0), weight_high)
    low_cell = jnp.maximum(low_cell, 0)
    weight_high = jnp.where(low_cell >= coarse_total - 1, jnp.float32(0.0), weight_high)
    low_cell = jnp.minimum(low_cell, coarse_total - 1)
    low_hit = (coarse_index[None, :] == low_cell[:, None]).astype(jnp.float32)
    high_hit = (coarse_index[None, :] == low_cell[:, None] + 1).astype(jnp.float32)
    return (1.0 - weight_high)[:, None] * low_hit + weight_high[:, None] * high_hit


def project(proj_weight, pooled):
    return jnp.einsum(
        "ck,cxyz->kxyz", proj_weight, pooled, preferred_element_type=jnp.float32
    ).astype(jnp.bfloat16)


def per_device(
    features,
    enc_weight,
    enc_bias,
    proj_weight,
    bottle_weight,
    bottle_bias,
    out_weight,
    dec_weight,
    dec_bias,
):
    channels, fine_x, merged = features.shape
    fine_z = FZ
    fine_y = merged // fine_z
    field = features.reshape(channels, fine_x, fine_y, fine_z)
    x_devices = lax.axis_size("sx")
    y_devices = lax.axis_size("sy")
    x_position = lax.axis_index("sx")
    y_position = lax.axis_index("sy")
    cells_x, cells_y, cells_z = (fine_x // POOL, fine_y // POOL, fine_z // POOL)
    extra = 1
    extended = padded_2(field, (("sx", 1), ("sy", 2)), extra + 1)
    encoded = jax.nn.relu(
        convolve(extended, enc_weight, 0, 0) + enc_bias[:, None, None, None]
    ).astype(jnp.bfloat16)
    own_part = encoded[:, extra : extra + fine_x, extra : extra + fine_y]
    pooled = jnp.max(
        own_part.reshape(channels, cells_x, POOL, cells_y, POOL, cells_z, POOL), axis=(2, 4, 6)
    )
    gathered = lax.all_gather(pooled, "sy", axis=2, tiled=True)
    projected = padded_2(project(proj_weight, gathered), (("sx", 1),), 1)
    bottleneck = jax.nn.relu(
        convolve(projected, bottle_weight, 0, 1) + bottle_bias[:, None, None, None]
    ).astype(jnp.bfloat16)
    partial_value = jnp.einsum(
        "kc,kxyz->cxyz", out_weight, bottleneck, preferred_element_type=jnp.float32
    )
    shared = lax.psum_scatter(partial_value, "sy", scatter_dimension=2, tiled=True)
    lowres = padded_2(shared, (("sx", 1), ("sy", 2)), 1)
    y_first = cells_y * y_position - 1
    y_count = cells_y + 2
    along_x = interpolate(
        fine_x + 2 * extra,
        fine_x * x_position - extra,
        cells_x + 2,
        cells_x * x_position - 1,
        cells_x * x_devices,
    )
    along_y = interpolate(
        fine_y + 2 * extra, fine_y * y_position - extra, y_count, y_first, cells_y * y_devices
    )
    along_z = interpolate(fine_z, 0, cells_z, 0, cells_z)
    highest = lax.Precision.HIGHEST
    step_one = jnp.einsum("kabc,zc->kabz", lowres, along_z, precision=highest)
    step_two = jnp.einsum("kabz,yb->kayz", step_one, along_y, precision=highest)
    upsampled = jnp.einsum("kayz,xa->kxyz", step_two, along_x, precision=highest)
    joined = (encoded.astype(jnp.float32) + upsampled).astype(jnp.bfloat16)
    global_x = fine_x * x_position - 1 + jnp.arange(fine_x + 2, dtype=jnp.int32)
    global_y = fine_y * y_position - 1 + jnp.arange(fine_y + 2, dtype=jnp.int32)
    inside_x = (global_x >= 0) & (global_x < fine_x * x_devices)
    inside_y = (global_y >= 0) & (global_y < fine_y * y_devices)
    inside = inside_x[:, None] & inside_y[None, :]
    padded = jnp.where(inside[None, :, :, None], joined, jnp.zeros((), jnp.bfloat16))
    decoded = (convolve(padded, dec_weight, 0, 0) + dec_bias[:, None, None, None]).astype(
        jnp.bfloat16
    )
    return decoded.reshape(channels, fine_x, merged)


def solution(mesh):
    in_specs = (
        P(None, "sx", "sy"),
        P(),
        P(),
        P(),
        P(None, None, None, "sy", None),
        P("sy"),
        P("sy", None),
        P(),
        P(),
    )
    out_specs = P(None, "sx", "sy")
    return jax.shard_map(
        per_device, mesh=mesh, in_specs=in_specs, out_specs=out_specs, check_vma=False
    )
```

profile of v0, /device:TPU:1, one launch (start us, length us, event | category | flops | bytes accessed | tf_op | source)
XLA Modules:
  0.0 105.4 jit_solution(12590503252826793971)
XLA Ops:
  0.0 2.2 %copy.50 = bf16[64,16,128]{0,2,1:T(8,128)(2,1)} copy(bf16[64,16,128]{2,1,0:T(8,128)(2,1)} %param.9) | data formatting | bytes 524288 | tf_op args[0]
  2.2 1.5 %fusion.91 = (bf16[64,2,8,16]{0,3,2,1:T(8,128)(2,1)}, bf16[64,2,8,16]{0,3,2,1:T(8,128)(2,1)}) fusion(bf16[64,16,8,16]{0,3,2,1:T(8,128)(2,1)} %bitcast.87), kind=kLoop, calls=%fused_computation.141 | loop fusion | bytes 131072 | tf_op jit(solution)/shard_map/slice | solution.py:18
  3.7 4.6 %collective-permute-start = (bf16[64,2,8,16]{0,3,2,1:T(8,128)(2,1)}, bf16[64,2,8,16]{0,3,2,1:T(8,128)(2,1)}, u32[]{:S(2)}, u32[]{:S(2)}) collective-permute-start(bf16[64,2,8,16]{0,3,2,1:T(8,128)(2,1)} %get-tuple-element.7), channel_id=1, source_target_pairs={{0,4},{4,8},{8,12},{12,16},{16,20},{20,24},{24,28},{1,5},{5,9},{9,... | collective-permute-start | bytes 98312 | tf_op jit(solution)/shard_map/ppermute | solution.py:20
  8.3 1.9 %collective-permute-start.1 = (bf16[64,2,8,16]{0,3,2,1:T(8,128)(2,1)}, bf16[64,2,8,16]{0,3,2,1:T(8,128)(2,1)}, u32[]{:S(2)}, u32[]{:S(2)}) collective-permute-start(bf16[64,2,8,16]{0,3,2,1:T(8,128)(2,1)} %get-tuple-element.8), channel_id=1, source_target_pairs={{4,0},{8,4},{12,8},{16,12},{20,16},{24,20},{28,24},{5,1},{9,5},{13... | collective-permute-start | bytes 98312 | tf_op jit(solution)/shard_map/ppermute | solution.py:21
  15.3 3.1 %collective-permute-start.2 = (bf16[64,20,2,16]{0,3,2,1:T(8,128)(2,1)S(1)}, bf16[64,20,2,16]{0,3,2,1:T(8,128)(2,1)S(1)}, u32[]{:S(2)}, u32[]{:S(2)}) collective-permute-start(bf16[64,20,2,16]{0,3,2,1:T(8,128)(2,1)S(1)} %get-tuple-element.5), channel_id=1, source_target_pairs={{0,1},{1,2},{2,3},{4,5},{5,6},{6,7},{8,9},{9,10},{10,11},{12,13},{... | collective-permute-start | bytes 245768 | tf_op jit(solution)/shard_map/ppermute | solution.py:20
  18.4 1.3 %collective-permute-start.3 = (bf16[64,20,2,16]{0,3,2,1:T(8,128)(2,1)S(1)}, bf16[64,20,2,16]{0,3,2,1:T(8,128)(2,1)S(1)}, u32[]{:S(2)}, u32[]{:S(2)}) collective-permute-start(bf16[64,20,2,16]{0,3,2,1:T(8,128)(2,1)S(1)} %get-tuple-element.6), channel_id=1, source_target_pairs={{1,0},{2,1},{3,2},{5,4},{6,5},{7,6},{9,8},{10,9},{11,10},{13,12},{... | collective-permute-start | bytes 245768 | tf_op jit(solution)/shard_map/ppermute | solution.py:21
  20.6 5.2 %collective-permute-done.3 = bf16[64,20,2,16]{0,3,2,1:T(8,128)(2,1)S(1)} collective-permute-done((bf16[64,20,2,16]{0,3,2,1:T(8,128)(2,1)S(1)}, bf16[64,20,2,16]{0,3,2,1:T(8,128)(2,1)S(1)}, u32[]{:S(2)}, u32[]{:S(2)}) %collective-permute-start.3) | collective-permute-done | bytes 81952 | tf_op jit(solution)/shard_map/ppermute | solution.py:21
  25.8 1.3 %maximum_bitcast_fusion = bf16[64,20,12,1,16]{0,4,2,1,3:T(8,128)(2,1)S(1)} fusion(bf16[64,20,2,16]{0,3,2,1:T(8,128)(2,1)S(1)} %collective-permute-done.3, bf16[64,2,8,16]{0,3,2,1:T(8,128)(2,1)} %collective-permute-done.1, bf16[64,16,8,16]{0,3,2,1:T(8,128)(2,1)} %bitcast.89, bf16[64,2,8,16]{0,3,2,1:T(8,128)(2,1)} %collective-permute-done, ...), kind=kLoop, calls=%fused_computation.33 | loop fusion | flops 983040 | bytes 983040 | tf_op jit(solution)/shard_map/broadcast_in_dim | solution.py:28
  29.2 8.6 %fusion.20 = f32[18,10,8,3,64]{4,2,3,1,0:T(8,128)S(1)} fusion(bf16[3,3,3,64,64]{4,3,2,1,0:T(8,128)(2,1)S(1)} %copy-done.6, bf16[64,20,12,1,7,2]{0,4,5,2,1,3:T(8,128)(2,1)S(1)} %slice.42, bf16[64,20,12,1,8,3]{0,4,5,2,1,3:T(8,128)(2,1)S(1)} %copy.53, pred[8,3]{0,1:T(4,128)(4,1)S(1)} %copy-done.8), kind=kOutput, calls=%fused_computation.22 | convolution fusion | flops 959477760 | bytes 2494488 | tf_op jit(solution)/shard_map/conv_general_dilated | solution.py:27
  41.6 6.0 %all-gather = bf16[64,2,8]{0,1,2:T(2,128)(2,1)S(1)} all-gather(bf16[64,2,2]{0,1,2:T(2,128)(2,1)S(1)} %copy.57), channel_id=2, replica_groups=mesh['sx'=8,'sy'=4] {'sy'}, dimensions={2}, use_global_device_ids=true | all-gather | bytes 2560 | tf_op jit(solution)/shard_map/all_gather | solution.py:88
  49.2 7.6 %collective-permute-start.4 = (bf16[512,1,4,2]{0,2,3,1:T(4,128)(2,1)}, bf16[512,1,4,2]{0,2,3,1:T(4,128)(2,1)}, u32[]{:S(2)}, u32[]{:S(2)}) collective-permute-start(bf16[512,1,4,2]{0,2,3,1:T(4,128)(2,1)} %get-tuple-element.9), channel_id=1, source_target_pairs={{0,4},{4,8},{8,12},{12,16},{16,20},{20,24},{24,28},{1,5},{5,9},{9,... | collective-permute-start | bytes 24584 | tf_op jit(solution)/shard_map/ppermute | solution.py:20
  56.7 2.1 %collective-permute-start.5 = (bf16[512,1,4,2]{0,2,3,1:T(4,128)(2,1)}, bf16[512,1,4,2]{0,2,3,1:T(4,128)(2,1)}, u32[]{:S(2)}, u32[]{:S(2)}) collective-permute-start(bf16[512,1,4,2]{0,2,3,1:T(4,128)(2,1)} %get-tuple-element.10), channel_id=1, source_target_pairs={{4,0},{8,4},{12,8},{16,12},{20,16},{24,20},{28,24},{5,1},{9,5},{13... | collective-permute-start | bytes 24584 | tf_op jit(solution)/shard_map/ppermute | solution.py:21
  60.7 1.3 %collective-permute-done.5 = bf16[512,1,4,2]{0,2,3,1:T(4,128)(2,1)} collective-permute-done((bf16[512,1,4,2]{0,2,3,1:T(4,128)(2,1)}, bf16[512,1,4,2]{0,2,3,1:T(4,128)(2,1)}, u32[]{:S(2)}, u32[]{:S(2)}) %collective-permute-start.5) | collective-permute-done | bytes 8224 | tf_op jit(solution)/shard_map/ppermute | solution.py:21
  64.2 7.1 %all-reduce = f32[64,2,4,2]{0,3,1,2:T(2,128)S(1)} all-reduce(f32[64,2,4,2]{0,3,1,2:T(2,128)S(1)} %copy.62), channel_id=3, replica_groups=mesh['sx'=8,'sy'=4] {'sy'}, use_global_device_ids=true, to_apply=%region_2.3.clone | all-reduce | flops 1024 | bytes 8192
  71.9 4.4 %collective-permute-start.6 = (f32[64,1,1,2]{0,3,2,1:T(2,128)S(1)}, f32[64,1,1,2]{0,3,2,1:T(2,128)S(1)}, u32[]{:S(2)}, u32[]{:S(2)}) collective-permute-start(f32[64,1,1,2]{0,3,2,1:T(2,128)S(1)} %get-tuple-element.11), channel_id=1, source_target_pairs={{0,4},{4,8},{8,12},{12,16},{16,20},{20,24},{24,28},{1,5},{5,9},{9,... | collective-permute-start | bytes 1544 | tf_op jit(solution)/shard_map/ppermute | solution.py:20
  76.2 1.9 %collective-permute-start.7 = (f32[64,1,1,2]{0,3,2,1:T(2,128)S(1)}, f32[64,1,1,2]{0,3,2,1:T(2,128)}, u32[]{:S(2)}, u32[]{:S(2)}) collective-permute-start(f32[64,1,1,2]{0,3,2,1:T(2,128)S(1)} %get-tuple-element.12), channel_id=1, source_target_pairs={{4,0},{8,4},{12,8},{16,12},{20,16},{24,20},{28,24},{5,1},{9,5},{13... | collective-permute-start | bytes 1544 | tf_op jit(solution)/shard_map/ppermute | solution.py:21
  78.7 2.5 %collective-permute-done.7 = f32[64,1,1,2]{0,3,2,1:T(2,128)} collective-permute-done((f32[64,1,1,2]{0,3,2,1:T(2,128)S(1)}, f32[64,1,1,2]{0,3,2,1:T(2,128)}, u32[]{:S(2)}, u32[]{:S(2)}) %collective-permute-start.7) | collective-permute-done | bytes 544 | tf_op jit(solution)/shard_map/ppermute | solution.py:21
  81.9 2.1 %collective-permute-start.8 = (f32[64,4,1,2]{0,3,2,1:T(2,128)S(1)}, f32[64,4,1,2]{0,3,2,1:T(2,128)S(1)}, u32[]{:S(2)}, u32[]{:S(2)}) collective-permute-start(f32[64,4,1,2]{0,3,2,1:T(2,128)S(1)} %pad_maximum_fusion.3), channel_id=1, source_target_pairs={{0,1},{1,2},{2,3},{4,5},{5,6},{6,7},{8,9},{9,10},{10,11},{12,13},{... | collective-permute-start | bytes 6152 | tf_op jit(solution)/shard_map/ppermute | solution.py:20
  84.0 1.3 %collective-permute-start.9 = (f32[64,4,1,2]{0,3,2,1:T(2,128)S(1)}, f32[64,4,1,2]{0,3,2,1:T(2,128)S(1)}, u32[]{:S(2)}, u32[]{:S(2)}) collective-permute-start(f32[64,4,1,2]{0,3,2,1:T(2,128)S(1)} %pad_maximum_fusion.3), channel_id=1, source_target_pairs={{1,0},{2,1},{3,2},{5,4},{6,5},{7,6},{9,8},{10,9},{11,10},{13,12},{... | collective-permute-start | bytes 6152 | tf_op jit(solution)/shard_map/ppermute | solution.py:21
  85.3 3.0 %collective-permute-done.9 = f32[64,4,1,2]{0,3,2,1:T(2,128)S(1)} collective-permute-done((f32[64,4,1,2]{0,3,2,1:T(2,128)S(1)}, f32[64,4,1,2]{0,3,2,1:T(2,128)S(1)}, u32[]{:S(2)}, u32[]{:S(2)}) %collective-permute-start.9) | collective-permute-done | bytes 2080 | tf_op jit(solution)/shard_map/ppermute | solution.py:21
  89.3 1.4 %convolution_bitcast_fusion = f32[64,4,10,16]{0,2,3,1:T(8,128)S(1)} fusion(f32[64,4,3,16]{0,3,2,1:T(8,128)S(1)} %fusion.37, f32[10]{0:T(128)} %get-tuple-element.17, s32[10]{0:T(128)} %get-tuple-element.20, f32[10]{0:T(128)} %get-tuple-element.18, s32[10]{0:T(128)} %get-tuple-element.19, s32[3]{0:T(128)} %iota_add_fusion), kind=kOutput, calls=%fused_computation.26 | convolution fusion | flops 1474710 | bytes 213164 | tf_op jit(solution)/shard_map/kabz,yb->kayz/dot_general | solution.py:113
  90.7 3.3 %fusion.27 = bf16[64,18,10,1,16]{0,1,4,2,3:T(8,128)(2,1)S(1)} fusion(bf16[64,18,10,16]{0,1,3,2:T(8,128)(2,1)} %copy-done.1, pred[18,10]{0,1:T(8,128)(4,1)} %broadcast_and_fusion, f32[64,4,10,16]{0,2,3,1:T(8,128)S(1)} %convolution_bitcast_fusion, f32[18]{0:T(128)} %get-tuple-element.13, s32[18]{0:T(128)} %get-tuple-element.16, f32[18]{0:T(128)} %get-tuple-element.14, ...), kind=kOutput, calls=%fused_computation.25 | convolution fusion | flops 9585000 | bytes 901604 | tf_op jit(solution)/shard_map/kayz,xa->kxyz/dot_general | solution.py:114
  95.3 6.1 %fusion.23 = f32[16,8,8,3,64]{4,2,3,1,0:T(8,128)S(1)} fusion(bf16[3,3,3,64,64]{4,3,2,1,0:T(8,128)(2,1)S(1)} %copy-done.7, bf16[64,18,10,1,7,2]{0,4,5,2,1,3:T(8,128)(2,1)S(1)} %slice.49, bf16[64,18,10,1,8,3]{0,4,5,2,1,3:T(8,128)(2,1)S(1)} %copy.69, pred[8,3]{0,1:T(4,128)(4,1)S(1)} %copy-done.9), kind=kOutput, calls=%fused_computation.23 | convolution fusion | flops 682438656 | bytes 1883160 | tf_op jit(solution)/shard_map/conv_general_dilated | solution.py:27
  103.4 2.0 %copy.72 = bf16[64,16,128]{2,1,0:T(8,128)(2,1)} copy(bf16[64,16,128]{0,2,1:T(8,128)(2,1)} %add_convert_fusion) | data formatting | bytes 524288 | tf_op jit(solution)/shard_map/convert_element_type | solution.py:122
  (67 shorter events, 23.2 us)
Async XLA Ops:
  0.0 62.8 %copy-start = (bf16[3,3,3,128,512]{4,3,2,1,0:T(8,128)(2,1)S(1)}, bf16[3,3,3,128,512]{4,3,2,1,0:T(8,128)(2,1)}, u32[]{:S(2)}) copy-start(bf16[3,3,3,128,512]{4,3,2,1,0:T(8,128)(2,1)} %param.13) | copy-start | bytes 10616836
  3.7 9.6 %collective-permute-start = (bf16[64,2,8,16]{0,3,2,1:T(8,128)(2,1)}, bf16[64,2,8,16]{0,3,2,1:T(8,128)(2,1)}, u32[]{:S(2)}, u32[]{:S(2)}) collective-permute-start(bf16[64,2,8,16]{0,3,2,1:T(8,128)(2,1)} %get-tuple-element.7), channel_id=1, source_target_pairs={{0,4},{4,8},{8,12},{12,16},{16,20},{20,24},{24,28},{1,5},{5,9},{9,... | collective-permute-start | bytes 98312 | tf_op jit(solution)/shard_map/ppermute | solution.py:20
  8.3 5.9 %collective-permute-start.1 = (bf16[64,2,8,16]{0,3,2,1:T(8,128)(2,1)}, bf16[64,2,8,16]{0,3,2,1:T(8,128)(2,1)}, u32[]{:S(2)}, u32[]{:S(2)}) collective-permute-start(bf16[64,2,8,16]{0,3,2,1:T(8,128)(2,1)} %get-tuple-element.8), channel_id=1, source_target_pairs={{4,0},{8,4},{12,8},{16,12},{20,16},{24,20},{28,24},{5,1},{9,5},{13... | collective-permute-start | bytes 98312 | tf_op jit(solution)/shard_map/ppermute | solution.py:21
  15.3 5.4 %collective-permute-start.2 = (bf16[64,20,2,16]{0,3,2,1:T(8,128)(2,1)S(1)}, bf16[64,20,2,16]{0,3,2,1:T(8,128)(2,1)S(1)}, u32[]{:S(2)}, u32[]{:S(2)}) collective-permute-start(bf16[64,20,2,16]{0,3,2,1:T(8,128)(2,1)S(1)} %get-tuple-element.5), channel_id=1, source_target_pairs={{0,1},{1,2},{2,3},{4,5},{5,6},{6,7},{8,9},{9,10},{10,11},{12,13},{... | collective-permute-start | bytes 245768 | tf_op jit(solution)/shard_map/ppermute | solution.py:20
  18.4 7.4 %collective-permute-start.3 = (bf16[64,20,2,16]{0,3,2,1:T(8,128)(2,1)S(1)}, bf16[64,20,2,16]{0,3,2,1:T(8,128)(2,1)S(1)}, u32[]{:S(2)}, u32[]{:S(2)}) collective-permute-start(bf16[64,20,2,16]{0,3,2,1:T(8,128)(2,1)S(1)} %get-tuple-element.6), channel_id=1, source_target_pairs={{1,0},{2,1},{3,2},{5,4},{6,5},{7,6},{9,8},{10,9},{11,10},{13,12},{... | collective-permute-start | bytes 245768 | tf_op jit(solution)/shard_map/ppermute | solution.py:21
  28.2 1.0 copy-start.6
  28.2 1.0 copy-start.8
  37.8 0.8 copy-start.3
  38.9 1.0 copy-start.1
  49.2 11.5 %collective-permute-start.4 = (bf16[512,1,4,2]{0,2,3,1:T(4,128)(2,1)}, bf16[512,1,4,2]{0,2,3,1:T(4,128)(2,1)}, u32[]{:S(2)}, u32[]{:S(2)}) collective-permute-start(bf16[512,1,4,2]{0,2,3,1:T(4,128)(2,1)} %get-tuple-element.9), channel_id=1, source_target_pairs={{0,4},{4,8},{8,12},{12,16},{16,20},{20,24},{24,28},{1,5},{5,9},{9,... | collective-permute-start | bytes 24584 | tf_op jit(solution)/shard_map/ppermute | solution.py:20
  56.7 5.3 %collective-permute-start.5 = (bf16[512,1,4,2]{0,2,3,1:T(4,128)(2,1)}, bf16[512,1,4,2]{0,2,3,1:T(4,128)(2,1)}, u32[]{:S(2)}, u32[]{:S(2)}) collective-permute-start(bf16[512,1,4,2]{0,2,3,1:T(4,128)(2,1)} %get-tuple-element.10), channel_id=1, source_target_pairs={{4,0},{8,4},{12,8},{16,12},{20,16},{24,20},{28,24},{5,1},{9,5},{13... | collective-permute-start | bytes 24584 | tf_op jit(solution)/shard_map/ppermute | solution.py:21
  62.8 1.2 %copy-start.5 = (f32[128]{0:T(128)S(1)}, f32[128]{0:T(128)}, u32[]{:S(2)}) copy-start(f32[128]{0:T(128)} %param.14) | copy-start | bytes 1540
  62.8 1.2 %copy-start.2 = (bf16[128,64]{0,1:T(8,128)(2,1)S(1)}, bf16[128,64]{0,1:T(8,128)(2,1)}, u32[]{:S(2)}) copy-start(bf16[128,64]{0,1:T(8,128)(2,1)} %param.15) | copy-start | bytes 49156
  71.9 6.8 %collective-permute-start.6 = (f32[64,1,1,2]{0,3,2,1:T(2,128)S(1)}, f32[64,1,1,2]{0,3,2,1:T(2,128)S(1)}, u32[]{:S(2)}, u32[]{:S(2)}) collective-permute-start(f32[64,1,1,2]{0,3,2,1:T(2,128)S(1)} %get-tuple-element.11), channel_id=1, source_target_pairs={{0,4},{4,8},{8,12},{12,16},{16,20},{20,24},{24,28},{1,5},{5,9},{9,... | collective-permute-start | bytes 1544 | tf_op jit(solution)/shard_map/ppermute | solution.py:20
  76.2 5.0 %collective-permute-start.7 = (f32[64,1,1,2]{0,3,2,1:T(2,128)S(1)}, f32[64,1,1,2]{0,3,2,1:T(2,128)}, u32[]{:S(2)}, u32[]{:S(2)}) collective-permute-start(f32[64,1,1,2]{0,3,2,1:T(2,128)S(1)} %get-tuple-element.12), channel_id=1, source_target_pairs={{4,0},{8,4},{12,8},{16,12},{20,16},{24,20},{28,24},{5,1},{9,5},{13... | collective-permute-start | bytes 1544 | tf_op jit(solution)/shard_map/ppermute | solution.py:21
  81.9 3.4 %collective-permute-start.8 = (f32[64,4,1,2]{0,3,2,1:T(2,128)S(1)}, f32[64,4,1,2]{0,3,2,1:T(2,128)S(1)}, u32[]{:S(2)}, u32[]{:S(2)}) collective-permute-start(f32[64,4,1,2]{0,3,2,1:T(2,128)S(1)} %pad_maximum_fusion.3), channel_id=1, source_target_pairs={{0,1},{1,2},{2,3},{4,5},{5,6},{6,7},{8,9},{9,10},{10,11},{12,13},{... | collective-permute-start | bytes 6152 | tf_op jit(solution)/shard_map/ppermute | solution.py:20
  84.0 4.4 %collective-permute-start.9 = (f32[64,4,1,2]{0,3,2,1:T(2,128)S(1)}, f32[64,4,1,2]{0,3,2,1:T(2,128)S(1)}, u32[]{:S(2)}, u32[]{:S(2)}) collective-permute-start(f32[64,4,1,2]{0,3,2,1:T(2,128)S(1)} %pad_maximum_fusion.3), channel_id=1, source_target_pairs={{1,0},{2,1},{3,2},{5,4},{6,5},{7,6},{9,8},{10,9},{11,10},{13,12},{... | collective-permute-start | bytes 6152 | tf_op jit(solution)/shard_map/ppermute | solution.py:21
  94.3 1.0 copy-start.7
  94.3 1.0 copy-start.9
  101.8 0.7 copy-start.4
where the time goes:
time: 106 us; the launch traced here: 105 us
  starting transfers between devices  30.2 us (28%)
  matrix products  22.7 us (21%)
  local copies, waits for them, and re-layouts  14.8 us (14%)
  waiting for transfers between devices  13.4 us (13%)
  blocking collectives  13.1 us (12%)
  other arithmetic  10.8 us (10%)
    ppermute x5, starting transfers between devices, padded_2(): before = lax.ppermute(last, axis, up)  21.7 us
    conv_general_dilated x3, matrix products, convolve(): lax.conv_general_dilated(padded[None], kernel, (1, 1, 1), ((pad_x, pad_x)...  15.9 us
    ppermute x5, waiting for transfers between devices, padded_2(): after = lax.ppermute(first, axis, down)  13 us
    ppermute x5, starting transfers between devices, padded_2(): after = lax.ppermute(first, axis, down)  8.53 us
    unnamed x1, blocking collectives  7.06 us
    unnamed x23, local copies, waits for them, and re-layouts  6.57 us
    all_gather x1, blocking collectives, per_device(): gathered = lax.all_gather(pooled, 'sy', axis=2, tiled=True)  6.01 us
    dot_general x1, matrix products, per_device(): jnp.einsum('kayz,xa->kxyz', step_two, along_x, precision=highest)  3.28 us
  transfers between devices with their start and end apart: 10, of which 6 were waited for; matrix products, arithmetic and copies ran while one was open for 6% of the time, Pallas kernels for 0%

commit v1 on v0

v1 whole, which is shorter than its diff:
```python
import functools

import jax
import jax.numpy as jnp
import numpy as np
from jax import lax
from jax.experimental import pallas as pl
from jax.experimental.pallas import tpu as pltpu
from jax.sharding import PartitionSpec as P

POOL = 8
FZ = 16
MESH = pl.DeviceIdType.MESH
BF = jnp.bfloat16
F32 = jnp.float32
SIDES = (-1, 0, 1)


def cell_selector(y_devices):
    outs = 4 * y_devices
    sel = np.zeros((27, outs, 3 * y_devices * 16), np.float32)
    for tap in range(27):
        a, b, c = tap // 9, tap // 3 % 3, tap % 3
        for row in range(outs):
            x, y, z = row // (2 * y_devices) + a - 1, row // 2 % y_devices + b - 1, row % 2 + c - 1
            if 0 <= y < y_devices and 0 <= z < 2:
                side, slot = ((0, 1), (1, 0), (1, 1), (2, 0))[x + 1]
                sel[tap, row, (side * y_devices + y) * 16 + slot * 2 + z] = 1
    return sel.reshape(27 * outs, -1)


def row_of(g, n):
    row = np.zeros(n)
    u = min(max((2 * g - 7) / 16, 0), n - 1)
    lo = int(np.floor(u))
    row[lo] += 1 - (u - lo)
    if lo + 1 < n:
        row[lo + 1] += u - lo
    return row


def plane_weights(y_devices, fine_y):
    total = y_devices * fine_y
    table = np.zeros((y_devices, fine_y + 2, FZ, y_devices, 2), np.float32)
    for s in range(y_devices):
        for y in range(fine_y + 2):
            g = min(max(s * fine_y + y - 1, 0), total - 1)
            table[s, y] = row_of(g, y_devices)[None, :, None] * np.stack([row_of(z, 2) for z in range(FZ)])[:, None, :]
    table = table.reshape(y_devices, (fine_y + 2) * FZ, -1)
    return np.concatenate([table] * 3, axis=2)


def dot_nt(a, b):
    return lax.dot_general(a, b, (((1,), (1,)), ((), ())), preferred_element_type=F32)


def dot(a, b):
    return jnp.dot(a, b, preferred_element_type=F32)


def arrange(w_ref, wm):
    ch = w_ref.shape[1]
    zero = jnp.zeros((ch, ch), BF)
    for bc in range(9):
        w0, w1, w2 = (w_ref[a * 9 + bc] for a in range(3))
        cols = pl.ds(bc * 2 * ch, 2 * ch)
        for n, (left, right) in enumerate(((w1, w2), (w0, w1), (zero, w0), (w2, zero))):
            wm[pl.ds(n * ch, ch), cols] = jnp.concatenate([left, right], axis=1)


def z_taps(value, z):
    rows = value.shape[0]
    below = jnp.where(z == 0, 0.0, pltpu.roll(value, 1, 0)).astype(BF)
    above = jnp.where(z == FZ - 1, 0.0, pltpu.roll(value, rows - 1, 0)).astype(BF)
    return below, value.astype(BF), above


def kernel(
    dims, f_ref, ew_ref, eb_ref, pw_ref, bw_hbm, bb_ref, ow_ref, dw_ref, db_ref, sel_ref, plane_ref, out_ref,
    f32s, base, taps, wm, wd, sums, enc, pooled, low, bw, halo_s, halo_r, pool_s, pool_r, low_s, low_r, bw_sem,
):
    nx, ny = dims
    ch, fx, lanes = f_ref.shape
    pairs = fx // 2
    rows = lanes
    wide = rows + 4 * FZ
    mid = rows + 2 * FZ
    ix, iy = lax.axis_index("sx"), lax.axis_index("sy")
    face = 2 * ny

    def there(d, e):
        ok = None
        for cond in ((ix > 0) if d < 0 else (ix < nx - 1) if d > 0 else None, (iy > 0) if e < 0 else (iy < ny - 1) if e > 0 else None):
            if cond is not None:
                ok = cond if ok is None else ok & cond
        return ok

    def partner(d, p):
        ok = there(d, 0)
        return (iy != p) if ok is None else ok

    weights = pltpu.make_async_copy(bw_hbm, bw, bw_sem)
    weights.start()

    barrier = pltpu.get_barrier_semaphore()
    for d in SIDES:
        for p in range(ny):
            @pl.when(partner(d, p))
            def _():
                pl.semaphore_signal(barrier, inc=1, device_id=(ix + d, p), device_id_type=MESH)

    f32s[...] = f_ref[...].astype(F32).reshape(ch * fx, lanes)
    for k in range(pairs):
        two = [f32s[pl.ds(2 * k + j, ch, stride=fx), :] for j in range(2)]
        base[k + 1, pl.ds(2 * FZ, rows), :] = jnp.concatenate(two, axis=0).T.astype(BF)

    present = (ix > 0).astype(jnp.int32) + (ix < nx - 1).astype(jnp.int32)
    pl.semaphore_wait(barrier, present * ny + ny - 1)

    def halo(d, e):
        src_k = pl.ds(1, pairs) if d == 0 else pl.ds(1 if d < 0 else pairs, 1)
        dst_k = pl.ds(1, pairs) if d == 0 else pl.ds(pairs + 1 if d < 0 else 0, 1)
        src_r = pl.ds(2 * FZ, rows) if e == 0 else pl.ds(2 * FZ if e < 0 else rows, 2 * FZ)
        dst_r = pl.ds(2 * FZ, rows) if e == 0 else pl.ds(rows + 2 * FZ if e < 0 else 0, 2 * FZ)
        n = (d + 1) * 3 + e + 1
        return pltpu.make_async_remote_copy(
            base.at[src_k, src_r], base.at[dst_k, dst_r], halo_s.at[n], halo_r.at[n],
            device_id=(ix + d, iy + e), device_id_type=MESH,
        )

    around = [(d, e) for d in SIDES for e in SIDES if d or e]
    for d, e in sorted(around, key=lambda de: (de[1] == 0, de[0] != 0)):
        @pl.when(there(d, e))
        def _():
            halo(d, e).start()

    arrange(ew_ref, wm)
    zeros_x = jnp.zeros((1, rows, 2 * ch), BF)
    zeros_y = jnp.zeros((pairs + 2, 2 * FZ, 2 * ch), BF)

    @pl.when(ix == 0)
    def _():
        base[pl.ds(0, 1), pl.ds(2 * FZ, rows), :] = zeros_x
        base[pl.ds(0, 1), pl.ds(0, 2 * FZ), :] = zeros_y[:1]
        base[pl.ds(0, 1), pl.ds(rows + 2 * FZ, 2 * FZ), :] = zeros_y[:1]
        pooled[0] = jnp.zeros(pooled.shape[1:], BF)

    @pl.when(ix == nx - 1)
    def _():
        base[pl.ds(pairs + 1, 1), pl.ds(2 * FZ, rows), :] = zeros_x
        base[pl.ds(pairs + 1, 1), pl.ds(0, 2 * FZ), :] = zeros_y[:1]
        base[pl.ds(pairs + 1, 1), pl.ds(rows + 2 * FZ, 2 * FZ), :] = zeros_y[:1]
        pooled[2] = jnp.zeros(pooled.shape[1:], BF)

    @pl.when(iy == 0)
    def _():
        base[:, pl.ds(0, 2 * FZ), :] = zeros_y

    @pl.when(iy == ny - 1)
    def _():
        base[:, pl.ds(rows + 2 * FZ, 2 * FZ), :] = zeros_y

    arrange(dw_ref, wd)

    for d, e in around:
        @pl.when(there(-d, -e))
        def _():
            halo(d, e).wait_recv()

    z_wide = lax.broadcasted_iota(jnp.int32, (wide, 2 * ch), 0) % FZ
    z_mid = lax.broadcasted_iota(jnp.int32, (mid, 2 * ch), 0) % FZ

    def encode(k, _):
        m, b, p = z_taps(base[k].astype(F32), z_wide)
        cols = [v[t * FZ : t * FZ + mid] for t in range(3) for v in (m, b, p)]
        sums[k] = dot_nt(jnp.concatenate(cols, axis=1), wm[...])
        return 0

    lax.fori_loop(0, pairs + 2, encode, 0)

    even = lax.broadcasted_iota(jnp.int32, (1, 2 * ch), 1) < ch

    def combine(k, count):
        tile = pl.ds(2 * ch, 2 * ch)
        before = sums[max(k - 1, 0), pl.ds(0, count), tile]
        after = sums[min(k + 1, pairs + 1), pl.ds(0, count), tile]
        return sums[k, pl.ds(0, count), pl.ds(0, 2 * ch)] + jnp.where(even, before, after)

    enc_bias = jnp.concatenate([eb_ref[...]] * 2, axis=1)
    best = []
    for k in list(range(1, pairs + 1)) + [0, pairs + 1]:
        value = jnp.maximum(combine(k, mid) + enc_bias, 0.0).astype(BF)
        enc[k] = value
        if 1 <= k <= pairs:
            own = value[FZ : FZ + rows].astype(F32).reshape(rows // FZ, 2, POOL, 2 * ch)
            own = jnp.max(own, axis=0)
            if (k - 1) % (POOL // 2) == 0:
                best.append(own)
            else:
                best[-1] = jnp.maximum(best[-1], own)
        if k == pairs:
            cells = [jnp.max(v, axis=1) for v in best]
            cells = jnp.concatenate(cells + [jnp.zeros((16 - 2 * len(cells), 2 * ch), F32)], axis=0)
            cells = jnp.maximum(cells, pltpu.roll(cells, ch, 1))
            pooled[1, iy] = cells.astype(BF)

            def pool_copy(d, p):
                return pltpu.make_async_remote_copy(
                    pooled.at[1, iy], pooled.at[1 - d, iy], pool_s.at[d + 1, p], pool_r.at[1 - d, iy],
                    device_id=(ix + d, p), device_id_type=MESH,
                )

            for d in (-1, 1, 0):
                for p in range(ny):
                    @pl.when(partner(d, p))
                    def _():
                        pool_copy(d, p).start()

    def pool_arrival(d, p):
        return pltpu.make_async_remote_copy(
            pooled.at[1, iy], pooled.at[d + 1, p], pool_s.at[d + 1, p], pool_r.at[d + 1, p],
            device_id=(ix + d, p), device_id_type=MESH,
        )

    weights.wait()
    for d in SIDES:
        for p in range(ny):
            @pl.when(partner(d, p))
            def _():
                pool_arrival(d, p).wait_recv()

    outs = 4 * ny
    cells = pooled[...].reshape(3 * ny * 16, 2 * ch)
    picked = dot(sel_ref[...], cells).astype(BF)[:, :ch]
    projected = dot(picked, pw_ref[...]).astype(BF)
    total = None
    for tap in range(27):
        term = dot_nt(projected[tap * outs : (tap + 1) * outs], bw[tap])
        total = term if total is None else total + term
    bottleneck = jnp.maximum(total + bb_ref[...], 0.0).astype(BF)
    share = dot(bottleneck, ow_ref[...])
    low[iy, 1:3] = jnp.concatenate([share, share], axis=1).reshape(2, face, 2 * ch)

    def low_copy(d, p, sender, receiver):
        src = pl.ds(1, 2) if d == 0 else pl.ds(1 if d < 0 else 2, 1)
        dst = pl.ds(1, 2) if d == 0 else pl.ds(3 if d < 0 else 0, 1)
        return pltpu.make_async_remote_copy(
            low.at[iy, src], low.at[sender, dst], low_s.at[d + 1, p], low_r.at[d + 1, receiver],
            device_id=(ix + d, p), device_id_type=MESH,
        )

    for d in (-1, 1, 0):
        for p in range(ny):
            @pl.when(partner(d, p))
            def _():
                low_copy(d, p, iy, iy).start()

    for d in SIDES:
        for p in range(ny):
            @pl.when(partner(-d, p))
            def _():
                low_copy(d, p, p, p).wait_recv()

    lowres = low[0]
    for s in range(1, ny):
        lowres = lowres + low[s]
    slots = [lowres[n] for n in range(4)]
    slots[0] = jnp.where(ix > 0, slots[0], slots[1])
    slots[3] = jnp.where(ix < nx - 1, slots[3], slots[2])
    rest = jnp.concatenate(slots, axis=1)
    parts = []
    for _ in range(3):
        part = rest.astype(BF).astype(F32)
        parts.append(part)
        rest = rest - part
    planes = dot(plane_ref[iy], jnp.concatenate(parts, axis=0).astype(BF))

    y_index = lax.broadcasted_iota(jnp.int32, (mid, 2 * ch), 0) // FZ
    inside = ((y_index > 0) | (iy > 0)) & ((y_index < rows // FZ + 1) | (iy < ny - 1))
    for k in range(pairs + 2):
        x = 2 * k - 2
        lo = (2 * x - 7) // (2 * POOL)
        w0, w1 = ((2 * (x + j) - 7 - 2 * POOL * lo) / (2 * POOL) for j in range(2))
        weight = jnp.where(even, F32(w0), F32(w1))
        first = planes[:, (lo + 1) * 2 * ch : (lo + 2) * 2 * ch]
        second = planes[:, (lo + 2) * 2 * ch : (lo + 3) * 2 * ch]
        up = (1.0 - weight) * first + weight * second
        joined = (enc[k].astype(F32) + up).astype(BF).astype(F32)
        keep = inside & (ix > 0) if k == 0 else inside & (ix < nx - 1) if k == pairs + 1 else inside
        m, b, p = z_taps(jnp.where(keep, joined, 0.0), z_mid)
        for t, v in enumerate((m, b, p)):
            taps[k, :, t * 2 * ch : (t + 1) * 2 * ch] = v

    def decode(k, _):
        cols = [taps[k, pl.ds(t * FZ, rows), :] for t in range(3)]
        sums[k, pl.ds(0, rows), :] = dot_nt(jnp.concatenate(cols, axis=1), wd[...])
        return 0

    lax.fori_loop(0, pairs + 2, decode, 0)

    dec_bias = jnp.concatenate([db_ref[...]] * 2, axis=1)
    for k in range(1, pairs + 1):
        value = (combine(k, rows) + dec_bias).T
        for j in range(2):
            f32s[pl.ds(2 * (k - 1) + j, ch, stride=fx), :] = value[j * ch : (j + 1) * ch]
    out_ref[...] = f32s[...].astype(BF).reshape(ch, fx, lanes)

    for d, e in around:
        @pl.when(there(d, e))
        def _():
            halo(d, e).wait_send()
    for d in SIDES:
        for p in range(ny):
            @pl.when(partner(d, p))
            def _():
                pool_arrival(d, p).wait_send()
                low_copy(d, p, iy, iy).wait_send()


def per_device(features, enc_weight, enc_bias, proj_weight, bottle_weight, bottle_bias, out_weight, dec_weight, dec_bias):
    channels, fine_x, merged = features.shape
    fine_y = merged // FZ
    if fine_x != 2 * POOL or fine_y != POOL:
        raise ValueError("block size")
    nx, ny = lax.axis_size("sx"), lax.axis_size("sy")
    filters, bottle = bottle_weight.shape[3:]
    pairs = fine_x // 2
    wide, mid = merged + 4 * FZ, merged + 2 * FZ
    c2 = 2 * channels
    vmem = pl.BlockSpec(memory_space=pltpu.VMEM)
    hbm = pl.BlockSpec(memory_space=pl.ANY)
    dma = pltpu.SemaphoreType.DMA
    return pl.pallas_call(
        functools.partial(kernel, (nx, ny)),
        out_shape=jax.ShapeDtypeStruct(features.shape, BF),
        in_specs=[vmem, vmem, vmem, vmem, hbm, vmem, vmem, vmem, vmem, vmem, vmem],
        out_specs=vmem,
        scratch_shapes=[
            pltpu.VMEM((channels * fine_x, merged), F32),
            pltpu.VMEM((pairs + 2, wide, c2), BF),
            pltpu.VMEM((pairs + 2, mid, 3 * c2), BF),
            pltpu.VMEM((2 * c2, 9 * c2), BF),
            pltpu.VMEM((2 * c2, 9 * c2), BF),
            pltpu.VMEM((pairs + 2, mid, 2 * c2), F32),
            pltpu.VMEM((pairs + 2, mid, c2), BF),
            pltpu.VMEM((3, ny, 16, c2), BF),
            pltpu.VMEM((ny, 4, 2 * ny, c2), F32),
            pltpu.VMEM((27, filters, bottle), BF),
            dma((9,)), dma((9,)), dma((3, ny)), dma((3, ny)), dma((3, ny)), dma((3, ny)), dma,
        ],
        compiler_params=pltpu.CompilerParams(
            collective_id=0, has_side_effects=True, vmem_limit_bytes=48 * 1024 * 1024
        ),
    )(
        features,
        enc_weight.reshape(27, channels, channels),
        enc_bias.reshape(1, channels),
        proj_weight,
        bottle_weight.reshape(27, filters, bottle),
        bottle_bias.reshape(1, filters),
        out_weight,
        dec_weight.reshape(27, channels, channels),
        dec_bias.reshape(1, channels),
        jnp.asarray(cell_selector(ny), BF),
        jnp.asarray(plane_weights(ny, fine_y), BF),
    )


def solution(mesh):
    in_specs = (
        P(None, "sx", "sy"), P(), P(), P(), P(None, None, None, "sy", None), P("sy"), P("sy", None), P(), P(),
    )
    return jax.shard_map(
        per_device, mesh=mesh, in_specs=in_specs, out_specs=P(None, "sx", "sy"), check_vma=False
    )
```

time: 106 us -> 38.3 us (0.36)
  starting transfers between devices: 30.2 us -> 0 us
  Pallas kernels: 0 us -> 26.7 us
  matrix products: 22.7 us -> 0 us
  waiting for transfers between devices: 13.4 us -> 0 us
  blocking collectives: 13.1 us -> 0 us
  other arithmetic: 10.8 us -> 0 us
  local copies, waits for them, and re-layouts: 14.8 us -> 11.2 us
    ppermute x10 -> x0, starting transfers between devices: 30.2 us -> none  [the longest x5 21.7 us: padded_2(): before = lax.ppermute(last, axis, up)]
    pallas_call x0 -> x1, Pallas kernels: none -> 26.7 us  [per_device(): pl.pallas_call(functools.partial(kernel, (nx, ny)), out_shape=jax.ShapeDt...]
    conv_general_dilated x3 -> x0, matrix products: 15.9 us -> none  [convolve(): lax.conv_general_dilated(padded[None], kernel, (1, 1, 1), ((pad_x, pad_x)...]
    ppermute x10 -> x0, waiting for transfers between devices: 13.4 us -> none  [the longest x5 13 us: padded_2(): after = lax.ppermute(first, axis, down)]
    unnamed x1 -> x0, blocking collectives: 7.06 us -> none
    dot_general x5 -> x0, matrix products: 6.74 us -> none  [the longest x1 3.28 us: per_device(): jnp.einsum('kayz,xa->kxyz', step_two, along_x, precision=highest)]
    all_gather x1 -> x0, blocking collectives: 6.01 us -> none  [per_device(): gathered = lax.all_gather(pooled, 'sy', axis=2, tiled=True)]
    unnamed x23 -> x22, local copies, waits for them, and re-layouts: 6.57 us -> 11.2 us
  transfers between devices with their start and end apart: 10 -> 0, of which waited for: 6 -> 0; matrix products, arithmetic and copies ran while one was open for 6% -> 0% of each run, Pallas kernels for 0% -> 0%
where the time goes in v1:
time: 38.3 us; the launch traced here: 37.9 us
  Pallas kernels  26.7 us (70%)
  local copies, waits for them, and re-layouts  11.2 us (29%)
    pallas_call x1, Pallas kernels, per_device(): pl.pallas_call(functools.partial(kernel, (nx, ny)), out_shape=jax.ShapeDt...  26.7 us
    unnamed x22, local copies, waits for them, and re-layouts  11.2 us

profile of v1, /device:TPU:1, one launch (start us, length us, event | category | flops | bytes accessed | tf_op | source)
XLA Modules:
  0.0 37.9 jit_solution(9215408012744609783)
XLA Ops:
  0.0 0.8 %copy.12.ow_ref = bf16[128,64]{1,0:T(8,128)(2,1)S(1)} copy(bf16[128,64]{0,1:T(8,128)(2,1)} %param.17) | data formatting | bytes 32768 | tf_op args[6]
  0.8 0.0 copy-start
  0.8 2.0 %copy-done = bf16[3,3,3,128,512]{4,3,2,1,0:T(8,128)(2,1)S(1)} copy-done((bf16[3,3,3,128,512]{4,3,2,1,0:T(8,128)(2,1)S(1)}, bf16[3,3,3,128,512]{4,3,2,1,0:T(8,128)(2,1)}, u32[]{:S(2)}) %copy-start) | copy-done | bytes 3538968
  2.8 0.0 copy-start.1
  2.8 1.0 %copy-done.1 = bf16[3,3,3,64,64]{4,3,2,1,0:T(8,128)(2,1)S(1)} copy-done((bf16[3,3,3,64,64]{4,3,2,1,0:T(8,128)(2,1)S(1)}, bf16[3,3,3,64,64]{4,3,2,1,0:T(8,128)(2,1)}, u32[]{:S(2)}) %copy-start.1) | copy-done | bytes 221208
  3.9 0.0 copy-start.2
  3.9 1.0 %copy-done.2 = bf16[3,3,3,64,64]{4,3,2,1,0:T(8,128)(2,1)S(1)} copy-done((bf16[3,3,3,64,64]{4,3,2,1,0:T(8,128)(2,1)S(1)}, bf16[3,3,3,64,64]{4,3,2,1,0:T(8,128)(2,1)}, u32[]{:S(2)}) %copy-start.2) | copy-done | bytes 221208
  4.9 0.0 copy-start.3
  4.9 0.9 %copy-done.3 = bf16[64,16,128]{2,1,0:T(8,128)(2,1)S(1)} copy-done((bf16[64,16,128]{2,1,0:T(8,128)(2,1)S(1)}, bf16[64,16,128]{2,1,0:T(8,128)(2,1)}, u32[]{:S(2)}) %copy-start.3) | copy-done | bytes 262168
  5.8 0.0 copy-start.4
  5.8 0.9 %copy-done.4 = bf16[432,192]{1,0:T(8,128)(2,1)S(1)} copy-done((bf16[432,192]{1,0:T(8,128)(2,1)S(1)}, bf16[432,192]{1,0:T(8,128)(2,1)}, u32[]{:S(2)}) %copy-start.4) | copy-done | bytes 165912
  6.8 0.0 copy-start.5
  6.8 0.9 %copy-done.5 = bf16[4,160,24]{2,1,0:T(8,128)(2,1)S(1)} copy-done((bf16[4,160,24]{2,1,0:T(8,128)(2,1)S(1)}, bf16[4,160,24]{2,1,0:T(8,128)(2,1)}, u32[]{:S(2)}) %copy-start.5) | copy-done | bytes 30744
  7.7 0.0 copy-start.6
  7.7 0.8 %copy-done.6 = bf16[64,512]{1,0:T(8,128)(2,1)S(1)} copy-done((bf16[64,512]{1,0:T(8,128)(2,1)S(1)}, bf16[64,512]{1,0:T(8,128)(2,1)}, u32[]{:S(2)}) %copy-start.6) | copy-done | bytes 65560
  8.5 0.0 copy-start.7
  8.5 0.7 %copy-done.7 = f32[64]{0:T(128)S(1)} copy-done((f32[64]{0:T(128)S(1)}, f32[64]{0:T(128)}, u32[]{:S(2)}) %copy-start.7) | copy-done | bytes 280
  9.2 0.0 copy-start.8
  9.2 0.7 %copy-done.8 = f32[128]{0:T(128)S(1)} copy-done((f32[128]{0:T(128)S(1)}, f32[128]{0:T(128)}, u32[]{:S(2)}) %copy-start.8) | copy-done | bytes 536
  9.8 0.0 copy-start.9
  9.8 0.7 %copy-done.9 = f32[64]{0:T(128)S(1)} copy-done((f32[64]{0:T(128)S(1)}, f32[64]{0:T(128)}, u32[]{:S(2)}) %copy-start.9) | copy-done | bytes 280
  10.5 26.7 %shard_map.109 = bf16[64,16,128]{2,1,0:T(8,128)(2,1)S(1)} custom-call(bf16[64,16,128]{2,1,0:T(8,128)(2,1)S(1)} %copy-done.3, bf16[27,64,64]{2,1,0:T(8,128)(2,1)S(1)} %bitcast.7, f32[1,64]{1,0:T(1,128)S(1)} %bitcast.9, bf16[64,512]{1,0:T(8,128)(2,1)S(1)} %copy-done.6, bf16[27,128,512]{2,1,0:T(8,128)(2,1)S(1)} %bitcast.6, f32[1,128]{1,0:T(1,128)S(1)} %bitcast.10, ...), custom_call_target="tpu_custom_call" | custom-call | tf_op jit(solution)/shard_map/pallas_call | solution.py:333
  37.2 0.7 %copy.14 = bf16[64,16,128]{2,1,0:T(8,128)(2,1)} copy(bf16[64,16,128]{2,1,0:T(8,128)(2,1)S(1)} %shard_map.109) | data formatting | bytes 524288
Async XLA Ops:
  0.8 2.0 %copy-start = (bf16[3,3,3,128,512]{4,3,2,1,0:T(8,128)(2,1)S(1)}, bf16[3,3,3,128,512]{4,3,2,1,0:T(8,128)(2,1)}, u32[]{:S(2)}) copy-start(bf16[3,3,3,128,512]{4,3,2,1,0:T(8,128)(2,1)} %param.15) | copy-start | bytes 10616836
  2.8 1.0 %copy-start.1 = (bf16[3,3,3,64,64]{4,3,2,1,0:T(8,128)(2,1)S(1)}, bf16[3,3,3,64,64]{4,3,2,1,0:T(8,128)(2,1)}, u32[]{:S(2)}) copy-start(bf16[3,3,3,64,64]{4,3,2,1,0:T(8,128)(2,1)} %param.12) | copy-start | bytes 663556
  3.9 1.0 %copy-start.2 = (bf16[3,3,3,64,64]{4,3,2,1,0:T(8,128)(2,1)S(1)}, bf16[3,3,3,64,64]{4,3,2,1,0:T(8,128)(2,1)}, u32[]{:S(2)}) copy-start(bf16[3,3,3,64,64]{4,3,2,1,0:T(8,128)(2,1)} %param.18) | copy-start | bytes 663556
  4.9 0.9 %copy-start.3 = (bf16[64,16,128]{2,1,0:T(8,128)(2,1)S(1)}, bf16[64,16,128]{2,1,0:T(8,128)(2,1)}, u32[]{:S(2)}) copy-start(bf16[64,16,128]{2,1,0:T(8,128)(2,1)} %f_ref.1) | copy-start | bytes 786436
  5.8 0.9 %copy-start.4 = (bf16[432,192]{1,0:T(8,128)(2,1)S(1)}, bf16[432,192]{1,0:T(8,128)(2,1)}, u32[]{:S(2)}) copy-start(bf16[432,192]{1,0:T(8,128)(2,1)} %constant.4.clone.sel_ref) | copy-start | bytes 497668
  6.8 0.9 %copy-start.5 = (bf16[4,160,24]{2,1,0:T(8,128)(2,1)S(1)}, bf16[4,160,24]{2,1,0:T(8,128)(2,1)}, u32[]{:S(2)}) copy-start(bf16[4,160,24]{2,1,0:T(8,128)(2,1)} %constant.5.clone.plane_ref) | copy-start | bytes 92164
  7.7 0.8 %copy-start.6 = (bf16[64,512]{1,0:T(8,128)(2,1)S(1)}, bf16[64,512]{1,0:T(8,128)(2,1)}, u32[]{:S(2)}) copy-start(bf16[64,512]{1,0:T(8,128)(2,1)} %pw_ref.1) | copy-start | bytes 196612
  8.5 0.7 %copy-start.7 = (f32[64]{0:T(128)S(1)}, f32[64]{0:T(128)}, u32[]{:S(2)}) copy-start(f32[64]{0:T(128)} %param.13) | copy-start | bytes 772
  9.2 0.7 %copy-start.8 = (f32[128]{0:T(128)S(1)}, f32[128]{0:T(128)}, u32[]{:S(2)}) copy-start(f32[128]{0:T(128)} %param.16) | copy-start | bytes 1540
  9.8 0.7 %copy-start.9 = (f32[64]{0:T(128)S(1)}, f32[64]{0:T(128)}, u32[]{:S(2)}) copy-start(f32[64]{0:T(128)} %param.19) | copy-start | bytes 772

commit v2 on v1

--- a/solution.py
+++ b/solution.py
@@ -76,8 +76,9 @@
 
 
 def kernel(
-    dims, f_ref, ew_ref, eb_ref, pw_ref, bw_hbm, bb_ref, ow_ref, dw_ref, db_ref, sel_ref, plane_ref, out_ref,
-    f32s, base, taps, wm, wd, sums, enc, pooled, low, bw, halo_s, halo_r, pool_s, pool_r, low_s, low_r, bw_sem,
+    dims, f_hbm, ew_hbm, eb_ref, pw_hbm, bw_hbm, bb_ref, ow_hbm, dw_hbm, db_ref, sel_hbm, plane_hbm, out_ref,
+    f32s, base, taps, wm, wd, sums, enc, pooled, low, f_ref, ew_ref, dw_ref, sel_ref, plane_ref, pw_ref, ow_ref, bw,
+    halo_s, halo_r, pool_s, pool_r, low_s, low_r, load_sem,
 ):
     nx, ny = dims
     ch, fx, lanes = f_ref.shape
@@ -99,8 +100,15 @@
         ok = there(d, 0)
         return (iy != p) if ok is None else ok
 
-    weights = pltpu.make_async_copy(bw_hbm, bw, bw_sem)
-    weights.start()
+    loads = [
+        pltpu.make_async_copy(src, dst, load_sem.at[n])
+        for n, (src, dst) in enumerate((
+            (f_hbm, f_ref), (ew_hbm, ew_ref), (dw_hbm, dw_ref), (sel_hbm, sel_ref),
+            (pw_hbm, pw_ref), (ow_hbm, ow_ref), (plane_hbm, plane_ref), (bw_hbm, bw),
+        ))
+    ]
+    for load in loads:
+        load.start()
 
     barrier = pltpu.get_barrier_semaphore()
     for d in SIDES:
@@ -109,6 +117,7 @@
             def _():
                 pl.semaphore_signal(barrier, inc=1, device_id=(ix + d, p), device_id_type=MESH)
 
+    loads[0].wait()
     f32s[...] = f_ref[...].astype(F32).reshape(ch * fx, lanes)
     for k in range(pairs):
         two = [f32s[pl.ds(2 * k + j, ch, stride=fx), :] for j in range(2)]
@@ -134,6 +143,7 @@
         def _():
             halo(d, e).start()
 
+    loads[1].wait()
     arrange(ew_ref, wm)
     zeros_x = jnp.zeros((1, rows, 2 * ch), BF)
     zeros_y = jnp.zeros((pairs + 2, 2 * FZ, 2 * ch), BF)
@@ -160,6 +170,7 @@
     def _():
         base[:, pl.ds(rows + 2 * FZ, 2 * FZ), :] = zeros_y
 
+    loads[2].wait()
     arrange(dw_ref, wd)
 
     for d, e in around:
@@ -222,7 +233,8 @@
             device_id=(ix + d, p), device_id_type=MESH,
         )
 
-    weights.wait()
+    for load in loads[3:]:
+        load.wait()
     for d in SIDES:
         for p in range(ny):
             @pl.when(partner(d, p))
@@ -238,7 +250,7 @@
         term = dot_nt(projected[tap * outs : (tap + 1) * outs], bw[tap])
         total = term if total is None else total + term
     bottleneck = jnp.maximum(total + bb_ref[...], 0.0).astype(BF)
-    share = dot(bottleneck, ow_ref[...])
+    share = dot_nt(bottleneck, ow_ref[...])
     low[iy, 1:3] = jnp.concatenate([share, share], axis=1).reshape(2, face, 2 * ch)
 
     def low_copy(d, p, sender, receiver):
@@ -327,13 +339,15 @@
     pairs = fine_x // 2
     wide, mid = merged + 4 * FZ, merged + 2 * FZ
     c2 = 2 * channels
+    selector = jnp.asarray(cell_selector(ny), BF)
+    planes = jnp.asarray(plane_weights(ny, fine_y), BF)
     vmem = pl.BlockSpec(memory_space=pltpu.VMEM)
     hbm = pl.BlockSpec(memory_space=pl.ANY)
     dma = pltpu.SemaphoreType.DMA
     return pl.pallas_call(
         functools.partial(kernel, (nx, ny)),
         out_shape=jax.ShapeDtypeStruct(features.shape, BF),
-        in_specs=[vmem, vmem, vmem, vmem, hbm, vmem, vmem, vmem, vmem, vmem, vmem],
+        in_specs=[hbm, hbm, vmem, hbm, hbm, vmem, hbm, hbm, vmem, hbm, hbm],
         out_specs=vmem,
         scratch_shapes=[
             pltpu.VMEM((channels * fine_x, merged), F32),
@@ -345,11 +359,18 @@
             pltpu.VMEM((pairs + 2, mid, c2), BF),
             pltpu.VMEM((3, ny, 16, c2), BF),
             pltpu.VMEM((ny, 4, 2 * ny, c2), F32),
+            pltpu.VMEM(features.shape, BF),
+            pltpu.VMEM((27, channels, channels), BF),
+            pltpu.VMEM((27, channels, channels), BF),
+            pltpu.VMEM(selector.shape, BF),
+            pltpu.VMEM(planes.shape, BF),
+            pltpu.VMEM(proj_weight.shape, BF),
+            pltpu.VMEM((channels, filters), BF),
             pltpu.VMEM((27, filters, bottle), BF),
-            dma((9,)), dma((9,)), dma((3, ny)), dma((3, ny)), dma((3, ny)), dma((3, ny)), dma,
+            dma((9,)), dma((9,)), dma((3, ny)), dma((3, ny)), dma((3, ny)), dma((3, ny)), dma((8,)),
         ],
         compiler_params=pltpu.CompilerParams(
-            collective_id=0, has_side_effects=True, vmem_limit_bytes=48 * 1024 * 1024
+            collective_id=0, has_side_effects=True, vmem_limit_bytes=63 * 1024 * 1024
         ),
     )(
         features,
@@ -358,11 +379,11 @@
         proj_weight,
         bottle_weight.reshape(27, filters, bottle),
         bottle_bias.reshape(1, filters),
-        out_weight,
+        out_weight.T,
         dec_weight.reshape(27, channels, channels),
         dec_bias.reshape(1, channels),
-        jnp.asarray(cell_selector(ny), BF),
-        jnp.asarray(plane_weights(ny, fine_y), BF),
+        selector,
+        planes,
     )
 
 

time: 38.3 us -> 29.5 us (0.77)
  local copies, waits for them, and re-layouts: 11.2 us -> 1.67 us
  Pallas kernels: 26.7 us -> 27.7 us
    unnamed x22 -> x1, local copies, waits for them, and re-layouts: 11.2 us -> 1.67 us
    pallas_call x1, Pallas kernels: 26.7 us -> 27.7 us  [per_device(): pl.pallas_call(functools.partial(kernel, (nx, ny)), out_shape=jax.ShapeDt...]
where the time goes in v2:
time: 29.5 us; the launch traced here: 29.4 us
  Pallas kernels  27.7 us (94%)
  local copies, waits for them, and re-layouts  1.67 us (6%)
    pallas_call x1, Pallas kernels, per_device(): pl.pallas_call(functools.partial(kernel, (nx, ny)), out_shape=jax.ShapeDt...  27.7 us
    unnamed x1, local copies, waits for them, and re-layouts  1.67 us

profile of v2, /device:TPU:1, one launch (start us, length us, event | category | flops | bytes accessed | tf_op | source)
XLA Modules:
  0.0 29.4 jit_solution(5400963638098106013)
XLA Ops:
  0.0 27.7 %shard_map.109 = bf16[64,16,128]{2,1,0:T(8,128)(2,1)} custom-call(bf16[64,16,128]{2,1,0:T(8,128)(2,1)} %f_hbm.1, bf16[27,64,64]{2,1,0:T(8,128)(2,1)} %bitcast.8, f32[1,64]{1,0:T(1,128)} %bitcast.11, bf16[64,512]{1,0:T(8,128)(2,1)} %pw_hbm.1, bf16[27,128,512]{2,1,0:T(8,128)(2,1)} %bitcast.7, f32[1,128]{1,0:T(1,128)} %bitcast.12, bf16[64,128]{1,0:T(8,128)(2,1)} %bitcast.10, ...), custom_call_target="tpu_custom_call" | custom-call | tf_op jit(solution)/shard_map/pallas_call | solution.py:347
  27.7 1.7 %copy.13 = bf16[64,16,128]{2,1,0:T(8,128)(2,1)} copy(bf16[64,16,128]{2,1,0:T(8,128)(2,1)} %shard_map.109) | data formatting | bytes 524288

commit v3 on v2

--- a/solution.py
+++ b/solution.py
@@ -63,9 +63,9 @@
     zero = jnp.zeros((ch, ch), BF)
     for bc in range(9):
         w0, w1, w2 = (w_ref[a * 9 + bc] for a in range(3))
-        cols = pl.ds(bc * 2 * ch, 2 * ch)
-        for n, (left, right) in enumerate(((w1, w2), (w0, w1), (zero, w0), (w2, zero))):
-            wm[pl.ds(n * ch, ch), cols] = jnp.concatenate([left, right], axis=1)
+        block = [jnp.concatenate(two, axis=1) for two in ((w1, w2), (w0, w1), (zero, w0), (w2, zero))]
+        block = jnp.concatenate(block, axis=0).astype(F32)
+        wm[pl.ds(bc * 2 * ch, 2 * ch), :] = block.T.astype(BF)
 
 
 def z_taps(value, z):
@@ -184,10 +184,10 @@
     def encode(k, _):
         m, b, p = z_taps(base[k].astype(F32), z_wide)
         cols = [v[t * FZ : t * FZ + mid] for t in range(3) for v in (m, b, p)]
-        sums[k] = dot_nt(jnp.concatenate(cols, axis=1), wm[...])
+        sums[k] = dot(jnp.concatenate(cols, axis=1), wm[...])
         return 0
 
-    lax.fori_loop(0, pairs + 2, encode, 0)
+    lax.fori_loop(0, pairs + 2, encode, 0, unroll=2)
 
     even = lax.broadcasted_iota(jnp.int32, (1, 2 * ch), 1) < ch
 
@@ -247,9 +247,9 @@
     projected = dot(picked, pw_ref[...]).astype(BF)
     total = None
     for tap in range(27):
-        term = dot_nt(projected[tap * outs : (tap + 1) * outs], bw[tap])
+        term = dot_nt(bw[tap], projected[tap * outs : (tap + 1) * outs])
         total = term if total is None else total + term
-    bottleneck = jnp.maximum(total + bb_ref[...], 0.0).astype(BF)
+    bottleneck = jnp.maximum(total.T + bb_ref[...], 0.0).astype(BF)
     share = dot_nt(bottleneck, ow_ref[...])
     low[iy, 1:3] = jnp.concatenate([share, share], axis=1).reshape(2, face, 2 * ch)
 
@@ -305,10 +305,10 @@
 
     def decode(k, _):
         cols = [taps[k, pl.ds(t * FZ, rows), :] for t in range(3)]
-        sums[k, pl.ds(0, rows), :] = dot_nt(jnp.concatenate(cols, axis=1), wd[...])
+        sums[k, pl.ds(0, rows), :] = dot(jnp.concatenate(cols, axis=1), wd[...])
         return 0
 
-    lax.fori_loop(0, pairs + 2, decode, 0)
+    lax.fori_loop(0, pairs + 2, decode, 0, unroll=2)
 
     dec_bias = jnp.concatenate([db_ref[...]] * 2, axis=1)
     for k in range(1, pairs + 1):
@@ -353,8 +353,8 @@
             pltpu.VMEM((channels * fine_x, merged), F32),
             pltpu.VMEM((pairs + 2, wide, c2), BF),
             pltpu.VMEM((pairs + 2, mid, 3 * c2), BF),
-            pltpu.VMEM((2 * c2, 9 * c2), BF),
-            pltpu.VMEM((2 * c2, 9 * c2), BF),
+            pltpu.VMEM((9 * c2, 2 * c2), BF),
+            pltpu.VMEM((9 * c2, 2 * c2), BF),
             pltpu.VMEM((pairs + 2, mid, 2 * c2), F32),
             pltpu.VMEM((pairs + 2, mid, c2), BF),
             pltpu.VMEM((3, ny, 16, c2), BF),

time: 29.5 us -> 26.7 us (0.905)
  Pallas kernels: 27.7 us -> 24.9 us
    pallas_call x1, Pallas kernels: 27.7 us -> 24.9 us  [per_device(): pl.pallas_call(functools.partial(kernel, (nx, ny)), out_shape=jax.ShapeDt...]
where the time goes in v3:
time: 26.7 us; the launch traced here: 26.5 us
  Pallas kernels  24.9 us (93%)
  local copies, waits for them, and re-layouts  1.67 us (6%)
    pallas_call x1, Pallas kernels, per_device(): pl.pallas_call(functools.partial(kernel, (nx, ny)), out_shape=jax.ShapeDt...  24.9 us
    unnamed x1, local copies, waits for them, and re-layouts  1.67 us

profile of v3, /device:TPU:1, one launch (start us, length us, event | category | flops | bytes accessed | tf_op | source)
XLA Modules:
  0.0 26.5 jit_solution(2462100710634539181)
XLA Ops:
  0.0 24.9 %shard_map.109 = bf16[64,16,128]{2,1,0:T(8,128)(2,1)} custom-call(bf16[64,16,128]{2,1,0:T(8,128)(2,1)} %f_hbm.1, bf16[27,64,64]{2,1,0:T(8,128)(2,1)} %bitcast.8, f32[1,64]{1,0:T(1,128)} %bitcast.11, bf16[64,512]{1,0:T(8,128)(2,1)} %pw_hbm.1, bf16[27,128,512]{2,1,0:T(8,128)(2,1)} %bitcast.7, f32[1,128]{1,0:T(1,128)} %bitcast.12, bf16[64,128]{1,0:T(8,128)(2,1)} %bitcast.10, ...), custom_call_target="tpu_custom_call" | custom-call | tf_op jit(solution)/shard_map/pallas_call | solution.py:347
  24.9 1.7 %copy.13 = bf16[64,16,128]{2,1,0:T(8,128)(2,1)} copy(bf16[64,16,128]{2,1,0:T(8,128)(2,1)} %shard_map.109) | data formatting | bytes 524288

commit v4 on v3

--- a/solution.py
+++ b/solution.py
@@ -181,13 +181,19 @@
     z_wide = lax.broadcasted_iota(jnp.int32, (wide, 2 * ch), 0) % FZ
     z_mid = lax.broadcasted_iota(jnp.int32, (mid, 2 * ch), 0) % FZ
 
-    def encode(k, _):
-        m, b, p = z_taps(base[k].astype(F32), z_wide)
-        cols = [v[t * FZ : t * FZ + mid] for t in range(3) for v in (m, b, p)]
-        sums[k] = dot(jnp.concatenate(cols, axis=1), wm[...])
+    group = (pairs + 2) // 2
+
+    def encode(g, _):
+        lhs = []
+        for n in range(group):
+            m, b, p = z_taps(base[g * group + n].astype(F32), z_wide)
+            cols = [v[t * FZ : t * FZ + mid] for t in range(3) for v in (m, b, p)]
+            lhs.append(jnp.concatenate(cols, axis=1))
+        value = dot(jnp.concatenate(lhs, axis=0), wm[...])
+        sums[pl.ds(g * group, group)] = value.reshape(group, mid, 4 * ch)
         return 0
 
-    lax.fori_loop(0, pairs + 2, encode, 0, unroll=2)
+    lax.fori_loop(0, 2, encode, 0)
 
     even = lax.broadcasted_iota(jnp.int32, (1, 2 * ch), 1) < ch
 
@@ -303,12 +309,16 @@
         for t, v in enumerate((m, b, p)):
             taps[k, :, t * 2 * ch : (t + 1) * 2 * ch] = v
 
-    def decode(k, _):
-        cols = [taps[k, pl.ds(t * FZ, rows), :] for t in range(3)]
-        sums[k, pl.ds(0, rows), :] = dot(jnp.concatenate(cols, axis=1), wd[...])
+    def decode(g, _):
+        lhs = []
+        for n in range(group):
+            cols = [taps[g * group + n, pl.ds(t * FZ, rows), :] for t in range(3)]
+            lhs.append(jnp.concatenate(cols, axis=1))
+        value = dot(jnp.concatenate(lhs, axis=0), wd[...])
+        sums[pl.ds(g * group, group), pl.ds(0, rows), :] = value.reshape(group, rows, 4 * ch)
         return 0
 
-    lax.fori_loop(0, pairs + 2, decode, 0, unroll=2)
+    lax.fori_loop(0, 2, decode, 0)
 
     dec_bias = jnp.concatenate([db_ref[...]] * 2, axis=1)
     for k in range(1, pairs + 1):

time: 26.7 us -> 25.6 us (0.959)
  Pallas kernels: 24.9 us -> 23.8 us
    pallas_call x1, Pallas kernels: 24.9 us -> 23.8 us  [per_device(): pl.pallas_call(functools.partial(kernel, (nx, ny)), out_shape=jax.ShapeDt...]
where the time goes in v4:
time: 25.6 us; the launch traced here: 25.5 us
  Pallas kernels  23.8 us (93%)
  local copies, waits for them, and re-layouts  1.67 us (7%)
    pallas_call x1, Pallas kernels, per_device(): pl.pallas_call(functools.partial(kernel, (nx, ny)), out_shape=jax.ShapeDt...  23.8 us
    unnamed x1, local copies, waits for them, and re-layouts  1.67 us

profile of v4, /device:TPU:1, one launch (start us, length us, event | category | flops | bytes accessed | tf_op | source)
XLA Modules:
  0.0 25.5 jit_solution(13598871909427886748)
XLA Ops:
  0.0 23.8 %shard_map.109 = bf16[64,16,128]{2,1,0:T(8,128)(2,1)} custom-call(bf16[64,16,128]{2,1,0:T(8,128)(2,1)} %f_hbm.1, bf16[27,64,64]{2,1,0:T(8,128)(2,1)} %bitcast.8, f32[1,64]{1,0:T(1,128)} %bitcast.11, bf16[64,512]{1,0:T(8,128)(2,1)} %pw_hbm.1, bf16[27,128,512]{2,1,0:T(8,128)(2,1)} %bitcast.7, f32[1,128]{1,0:T(1,128)} %bitcast.12, bf16[64,128]{1,0:T(8,128)(2,1)} %bitcast.10, ...), custom_call_target="tpu_custom_call" | custom-call | tf_op jit(solution)/shard_map/pallas_call | solution.py:357
  23.8 1.7 %copy.13 = bf16[64,16,128]{2,1,0:T(8,128)(2,1)} copy(bf16[64,16,128]{2,1,0:T(8,128)(2,1)} %shard_map.109) | data formatting | bytes 524288
